TPU v7x, 1024 devices: a whole 4x8x16 slice. The times are simulated.
1024 devices in a mesh: gx: 16 (over z_lo, core), gy: 8 (over y), gz: 8 (over x, z_hi).
Axes of the slice: x: 4, y: 8, z: 16 (z_hi: 2, z_lo: 8; z = z_hi * 8 + z_lo), core: 2. Of those that a mesh axis runs over, the one named last changes fastest.
Arguments:
- positions: float32 [16, 8, 8, 3, 128], P('gx', 'gy', 'gz'), may hold values from 0 to 10
- species: int32 [16, 8, 8, 128], P('gx', 'gy', 'gz'), may hold values from 0 to 7
- send_list: int32 [16, 8, 8, 2, 64], P('gx', 'gy', 'gz'), may hold values from 0 to 127, as said below
- send_count: int32 [16, 8, 8, 2], P('gx', 'gy', 'gz'), may hold values from 1 to 64, as said below
- pair_list: int32 [16, 8, 8, 8, 2], P('gx', 'gy', 'gz'), may hold values from 0 to 107, as said below
- pair_count: int32 [16, 8, 8], P('gx', 'gy', 'gz'), may hold values from 1 to 8, as said below
- w_radial: float32 [8, 64], replicated, may hold values from -2 to 2
- species_emb: float32 [8, 64], replicated, may hold values from -4 to 4
- w_first: bfloat16 [256, 512], replicated, may hold values from -0.375 to 0.375
- w_second: bfloat16 [512, 512], replicated, may hold values from -0.25 to 0.25
- w_out: float32 [512], replicated, may hold values from -0.25 to 0.25
Outputs:
- forces: float32 [16, 8, 8, 3, 256], P('gx', 'gy', 'gz')
- atom_energy: float32 [16, 8, 8, 256], P('gx', 'gy', 'gz')
Inputs may be any that keep to these rules, and one draw needn't show every extreme that they name: `send_list`: within one cell the first send_count entries of both lists together name distinct atoms. `send_count`: some cell fills a list. `pair_list`: column 0 is below 4; only the first pair_count rows of a cell are used. `pair_count`: some cell uses all slots.
All inputs are finite; a program needn't handle non-finite values.
Results may differ from a plain program's by a relative error of at most 0.018.
Values sent between devices are 32-bit elements; how exact they have to be, the bound alone decides.
A program may use at most 32 MiB of HBM per device.

v0:
```python
import jax
import jax.numpy as jnp
from jax import lax
from jax.sharding import PartitionSpec as P

TILE = 64
NB = 8
SPECIES = 8


cell = 10.0
cutoff = 5.0
cutoff_sq = 25.0
soften = 0.25
sharpness = 1.0
env_scale = 0.5


def from_behind(value, axis, steps):
    count = lax.axis_size(axis)
    pairs = [(source, (source + steps) % count) for source in range(count)]
    return lax.ppermute(value, axis, pairs)


def with_halo(cells, sides, width):
    for axis, dim in sides:
        count = lax.axis_size(axis)
        head = lax.slice_in_dim(cells, 0, width, axis=dim)
        tail = lax.slice_in_dim(cells, cells.shape[dim] - width, cells.shape[dim], axis=dim)
        cells = jnp.concatenate(
            [
                lax.ppermute(tail, axis, [(i, (i + 1) % count) for i in range(count)]),
                cells,
                lax.ppermute(head, axis, [((i + 1) % count, i) for i in range(count)]),
            ],
            axis=dim,
        )
    return cells


def offsets_grid():
    stepping = (jnp.arange(3, dtype=jnp.float32) - 1.0) * cell
    zeroes = jnp.zeros((3, 3, 3), jnp.float32)
    return jnp.stack(
        [
            zeroes + stepping[:, None, None],
            zeroes + stepping[None, :, None],
            zeroes + stepping[None, None, :],
        ],
        3,
    )[..., None]


def depart(packed, lists, counts):
    capacity = lists.shape[-1]
    live_slot = jnp.arange(capacity)[None, :] < counts[:, None]
    buffers = packed[:, lists]
    kind_row = jnp.where(live_slot[None], buffers[3:4], -1.0)
    buffers = jnp.concatenate([buffers[:3], kind_row], 0)
    leaving = (lists[:, :, None] == jnp.arange(packed.shape[1])[None, None, :]) & live_slot[
        :, :, None
    ]
    leaving = jnp.any(leaving, axis=(0, 1))
    staying = jnp.concatenate([packed[:3], jnp.where(leaving, -1.0, packed[3])[None]], 0)
    return (buffers[:, 0], buffers[:, 1], staying)


def tile_environment(centre_tile, other_tile, same_tile, w_radial, species_emb):
    delta = other_tile[:3, None, :] - centre_tile[:3, :, None]
    squared = jnp.sum(delta * delta, axis=0)
    distance = jnp.sqrt(squared + soften)
    unit_x = delta[0] / distance
    unit_y = delta[1] / distance
    unit_z = delta[2] / distance
    both_live = (centre_tile[3] >= 0).astype(jnp.float32)[:, None] * (other_tile[3] >= 0).astype(
        jnp.float32
    )[None, :]
    diagonal = jnp.eye(TILE, dtype=jnp.float32) * same_tile.astype(jnp.float32)
    inside = jnp.maximum(1.0 - squared / cutoff_sq, 0.0)
    envelope = inside * inside * both_live * (1.0 - diagonal)
    centres = (jnp.arange(NB, dtype=jnp.float32) + 1.0) * (cutoff / NB)
    radial_basis = (
        jnp.exp(-sharpness * (distance[:, :, None] - centres) ** 2) * envelope[:, :, None]
    )
    harmonics = jnp.stack(
        [
            jnp.ones_like(unit_x),
            unit_x,
            unit_y,
            unit_z,
            unit_x * unit_y,
            unit_y * unit_z,
            1.5 * unit_z * unit_z - 0.5,
            unit_x * unit_z,
            0.5 * (unit_x * unit_x - unit_y * unit_y),
        ],
        -1,
    )
    mixed = (radial_basis[:, :, :, None] * harmonics[:, :, None, :]).reshape(TILE, TILE, NB * 9)
    species_hot = (
        other_tile[3][:, None] == jnp.arange(SPECIES, dtype=jnp.float32)[None, :]
    ).astype(jnp.float32)
    neighbour_embed = jnp.dot(species_hot, species_emb, precision=lax.Precision.HIGHEST)
    gathered = jnp.einsum("ijx,jc->ixc", mixed, neighbour_embed, precision=lax.Precision.HIGHEST)
    gathered = gathered.reshape(TILE, NB, 9, -1)
    return jnp.einsum("inmc,nc->icm", gathered, w_radial, precision=lax.Precision.HIGHEST)


def local_energy(extended, pair_rows, pair_total, w_radial, species_emb, w_first, w_second, w_out):
    width = extended.shape[-1]
    tile_count = width // TILE
    channels = species_emb.shape[1]
    pieces = (
        extended.reshape(27, 4, tile_count, TILE)
        .transpose(0, 2, 1, 3)
        .reshape(27 * tile_count, 4, TILE)
    )
    centre_base = 13 * tile_count
    visit_tile = jax.checkpoint(tile_environment)

    def visit(running, entry):
        pair_row, position = entry
        centre_index = centre_base + pair_row[0]
        contribution = visit_tile(
            pieces[centre_index],
            pieces[pair_row[1]],
            pair_row[1] == centre_index,
            w_radial,
            species_emb,
        )
        active = (position < pair_total).astype(jnp.float32)
        select = (jnp.arange(tile_count) == pair_row[0]).astype(jnp.float32) * active
        return (running + select[:, None, None, None] * contribution[None], None)

    start_env = jnp.zeros((tile_count, TILE, channels, 9), jnp.float32)
    environment, _ = lax.scan(visit, start_env, (pair_rows, jnp.arange(pair_rows.shape[0])))
    environment = environment.reshape(width, channels, 9) * env_scale
    invariants = jnp.concatenate(
        [
            environment[:, :, 0] ** 2,
            jnp.sum(environment[:, :, 1:4] ** 2, -1),
            jnp.sum(environment[:, :, 4:] ** 2, -1),
        ],
        -1,
    )
    centre_kinds = extended[13, 3]
    centre_live = (centre_kinds >= 0).astype(jnp.float32)
    centre_hot = (centre_kinds[:, None] == jnp.arange(SPECIES, dtype=jnp.float32)[None, :]).astype(
        jnp.float32
    )
    centre_embed = jnp.dot(centre_hot, species_emb, precision=lax.Precision.HIGHEST)
    features = jnp.concatenate([invariants, centre_embed], -1).astype(jnp.bfloat16)
    first_layer = jax.nn.silu(
        jnp.dot(features, w_first, preferred_element_type=jnp.float32)
    ).astype(jnp.bfloat16)
    second_layer = jax.nn.silu(
        jnp.dot(first_layer, w_second, preferred_element_type=jnp.float32)
    ).astype(jnp.bfloat16)
    return (
        jnp.dot(second_layer.astype(jnp.float32), w_out, precision=lax.Precision.HIGHEST)
        * centre_live
    )


def local(
    positions,
    species,
    send_list,
    send_count,
    pair_list,
    pair_count,
    w_radial,
    species_emb,
    w_first,
    w_second,
    w_out,
):
    packed = jnp.concatenate([positions[0, 0, 0], species[0, 0, 0].astype(jnp.float32)[None, :]], 0)
    to_lower, to_upper, staying = depart(packed, send_list[0, 0, 0], send_count[0, 0, 0])
    arrived = []
    for stride, outgoing in ((1, to_upper), (-1, to_lower)):
        landed = from_behind(outgoing, "gx", stride)
        arrived.append(landed.at[0].add(-stride * cell))
    fresh = jnp.concatenate([arrived[0], staying, arrived[1]], 1)
    own_block = fresh[None, None, None]
    beside_all = with_halo(own_block, (("gx", 0), ("gy", 1), ("gz", 2)), 1)
    coords = beside_all[:, :, :, :3] + offsets_grid()
    kinds = beside_all[:, :, :, 3:4]
    pair_rows = pair_list[0, 0, 0]
    pair_total = pair_count.reshape(())

    def energy_of(coordinates):
        extended = jnp.concatenate([coordinates, kinds], 3).reshape(27, 4, -1)
        return local_energy(
            extended, pair_rows, pair_total, w_radial, species_emb, w_first, w_second, w_out
        )

    energies, pullback = jax.vjp(energy_of, coords)
    (gradient,) = pullback(jnp.ones_like(energies))
    padded = with_halo(gradient, (("gx", 0), ("gy", 1), ("gz", 2)), 1)
    summed = jnp.sum(padded[0::2, 0::2, 0::2], axis=(0, 1, 2))
    return ((-summed)[None, None, None], energies[None, None, None])


def solution(mesh):
    placed = (
        P("gx", "gy", "gz", None, None),
        P("gx", "gy", "gz", None),
        P("gx", "gy", "gz", None, None),
        P("gx", "gy", "gz", None),
        P("gx", "gy", "gz", None, None),
        P("gx", "gy", "gz"),
        P(),
        P(),
        P(),
        P(),
        P(),
    )
    return jax.shard_map(
        local,
        mesh=mesh,
        in_specs=placed,
        out_specs=(P("gx", "gy", "gz", None, None), P("gx", "gy", "gz", None)),
        check_vma=False,
    )
```

profile of v0, /device:TPU:8, one launch (start us, length us, event | category | flops | bytes accessed | tf_op | source)
XLA Modules:
  0.0 398.8 jit_solution(12985195735550124101)
XLA Ops:
  4.4 15.8 %collective-permute-start.1 = (f32[4,64]{1,0:T(4,128)S(1)}, f32[4,64]{1,0:T(4,128)S(1)}, u32[]{:S(2)}, u32[]{:S(2)}) collective-permute-start(f32[4,64]{1,0:T(4,128)S(1)} %get-tuple-element.673), channel_id=1, source_target_pairs={{0,960},{64,0},{128,64},{192,128},{256,192},{320,256},{384,320},{4... | collective-permute-start | bytes 3080 | tf_op jit(solution)/shard_map/ppermute | solution.py:22
  20.2 1.9 collective-permute-start
  24.3 7.4 %collective-permute-done = f32[4,64]{1,0:T(4,128)S(1)} collective-permute-done((f32[4,64]{1,0:T(4,128)S(1)}, f32[4,64]{1,0:T(4,128)S(1)}, u32[]{:S(2)}, u32[]{:S(2)}) %collective-permute-start) | collective-permute-done | bytes 1056 | tf_op jit(solution)/shard_map/ppermute | solution.py:22
  31.9 2.9 collective-permute-start.3
  34.7 1.9 collective-permute-start.2
  36.7 9.6 %collective-permute-done.2 = f32[1,1,1,4,256]{4,3,2,1,0:T(4,128)S(1)} collective-permute-done((f32[1,1,1,4,256]{4,3,2,1,0:T(4,128)S(1)}, f32[1,1,1,4,256]{4,3,2,1,0:T(4,128)S(1)}, u32[]{:S(2)}, u32[]{:S(2)}) %collective-permute-start.2) | collective-permute-done | bytes 4128 | tf_op jit(solution)/shard_map/ppermute | solution.py:32
  46.3 2.3 collective-permute-start.5
  48.6 3.5 collective-permute-start.4
  52.2 3.5 collective-permute-done.4
  55.7 11.9 %collective-permute-start.6 = (f32[3,3,1,4,256]{4,3,2,1,0:T(4,128)S(1)}, f32[3,3,1,4,256]{4,3,2,1,0:T(4,128)S(1)}, u32[]{:S(2)}, u32[]{:S(2)}) collective-permute-start(f32[3,3,1,4,256]{4,3,2,1,0:T(4,128)S(1)} %pad_maximum_fusion.15), channel_id=1, source_target_pairs={{0,1},{1,2},{2,3},{3,4},{4,5},{5,6},{6,7},{7,0},{8,9},{9,10},{10,1... | collective-permute-start | bytes 110600 | tf_op jit(solution)/shard_map/ppermute | solution.py:32
  67.6 4.8 %collective-permute-start.7 = (f32[3,3,1,4,256]{4,3,2,1,0:T(4,128)S(1)}, f32[3,3,1,4,256]{4,3,2,1,0:T(4,128)S(1)}, u32[]{:S(2)}, u32[]{:S(2)}) collective-permute-start(f32[3,3,1,4,256]{4,3,2,1,0:T(4,128)S(1)} %pad_maximum_fusion.15), channel_id=1, source_target_pairs={{1,0},{2,1},{3,2},{4,3},{5,4},{6,5},{7,6},{0,7},{9,8},{10,9},{11,1... | collective-permute-start | bytes 110600 | tf_op jit(solution)/shard_map/ppermute | solution.py:34
  72.8 9.4 %collective-permute-done.7 = f32[3,3,1,4,256]{4,3,2,1,0:T(4,128)S(1)} collective-permute-done((f32[3,3,1,4,256]{4,3,2,1,0:T(4,128)S(1)}, f32[3,3,1,4,256]{4,3,2,1,0:T(4,128)S(1)}, u32[]{:S(2)}, u32[]{:S(2)}) %collective-permute-start.7) | collective-permute-done | bytes 36896 | tf_op jit(solution)/shard_map/ppermute | solution.py:34
  82.5 100.7 %while.42 = (s32[]{:T(128)}, f32[4,64,64,9]{2,1,3,0:T(8,128)S(1)}, s32[8]{0:T(128)S(1)}, s32[8]{0:T(128)S(1)}, f32[8,4,64]{2,1,0:T(4,128)S(1)}, /*index=5*/f32[8...) while((s32[]{:T(128)}, f32[4,64,64,9]{2,1,3,0:T(8,128)S(1)}, ...), condition=%wide.region_3.4_spmd.clone, body=%wide.region_1.3_spmd.clone.sunk | while | flops 228508448 | bytes 3039461 | solution.py:136
  89.3 2.7 multiply_reduce_fusion.15
  101.8 2.7 multiply_reduce_fusion.15
  114.4 2.7 multiply_reduce_fusion.15
  127.0 2.7 multiply_reduce_fusion.15
  139.6 2.7 multiply_reduce_fusion.15
  152.2 2.7 multiply_reduce_fusion.15
  164.8 2.7 multiply_reduce_fusion.15
  177.4 2.7 multiply_reduce_fusion.15
  184.8 1.9 mul.1138
  190.8 155.9 %while.41 = (s32[]{:T(128)}, f32[108,4,64]{2,1,0:T(4,128)S(1)}, s32[8]{0:T(128)S(1)}, f32[8,4,64]{2,1,0:T(4,128)S(1)}, f32[8,4,64]{2,1,0:T(4,128)S(1)}, /*index=...) while((s32[]{:T(128)}, f32[108,4,64]{2,1,0:T(4,128)S(1)}, ...), condition=%wide.region_15.16_spmd, body=%wide.region_6.0_spmd.sunk | while | flops 229753936 | bytes 10679388 | solution.py:136
  194.3 8.7 %fusion.185 = f32[64,64,72]{2,1,0:T(8,128)} fusion(f32[64,64,1]{1,0,2:T(8,128)S(1)} %convolution_bitcast_fusion.4, f32[64,72,64]{2,0,1:T(8,128)S(1)} %bitcast.610), kind=kOutput, calls=%fused_computation.9.clone.1 | convolution fusion | flops 226492416 | bytes 2375680 | tf_op jit(solution)/shard_map/transpose(jvp())/while/body/eval_jaxpr/checkpoint/ijx,jc->ixc/dot_general | solution.py:104
  202.9 3.3 copy.79
  213.7 8.7 %fusion.185 = f32[64,64,72]{2,1,0:T(8,128)} fusion(f32[64,64,1]{1,0,2:T(8,128)S(1)} %convolution_bitcast_fusion.4, f32[64,72,64]{2,0,1:T(8,128)S(1)} %bitcast.610), kind=kOutput, calls=%fused_computation.9.clone.1 | convolution fusion | flops 226492416 | bytes 2375680 | tf_op jit(solution)/shard_map/transpose(jvp())/while/body/eval_jaxpr/checkpoint/ijx,jc->ixc/dot_general | solution.py:104
  222.4 3.3 copy.79
  233.2 8.7 %fusion.185 = f32[64,64,72]{2,1,0:T(8,128)} fusion(f32[64,64,1]{1,0,2:T(8,128)S(1)} %convolution_bitcast_fusion.4, f32[64,72,64]{2,0,1:T(8,128)S(1)} %bitcast.610), kind=kOutput, calls=%fused_computation.9.clone.1 | convolution fusion | flops 226492416 | bytes 2375680 | tf_op jit(solution)/shard_map/transpose(jvp())/while/body/eval_jaxpr/checkpoint/ijx,jc->ixc/dot_general | solution.py:104
  241.8 3.3 copy.79
  252.6 8.7 %fusion.185 = f32[64,64,72]{2,1,0:T(8,128)} fusion(f32[64,64,1]{1,0,2:T(8,128)S(1)} %convolution_bitcast_fusion.4, f32[64,72,64]{2,0,1:T(8,128)S(1)} %bitcast.610), kind=kOutput, calls=%fused_computation.9.clone.1 | convolution fusion | flops 226492416 | bytes 2375680 | tf_op jit(solution)/shard_map/transpose(jvp())/while/body/eval_jaxpr/checkpoint/ijx,jc->ixc/dot_general | solution.py:104
  261.3 3.3 copy.79
  272.1 8.7 %fusion.185 = f32[64,64,72]{2,1,0:T(8,128)} fusion(f32[64,64,1]{1,0,2:T(8,128)S(1)} %convolution_bitcast_fusion.4, f32[64,72,64]{2,0,1:T(8,128)S(1)} %bitcast.610), kind=kOutput, calls=%fused_computation.9.clone.1 | convolution fusion | flops 226492416 | bytes 2375680 | tf_op jit(solution)/shard_map/transpose(jvp())/while/body/eval_jaxpr/checkpoint/ijx,jc->ixc/dot_general | solution.py:104
  280.8 3.3 copy.79
  291.6 8.7 %fusion.185 = f32[64,64,72]{2,1,0:T(8,128)} fusion(f32[64,64,1]{1,0,2:T(8,128)S(1)} %convolution_bitcast_fusion.4, f32[64,72,64]{2,0,1:T(8,128)S(1)} %bitcast.610), kind=kOutput, calls=%fused_computation.9.clone.1 | convolution fusion | flops 226492416 | bytes 2375680 | tf_op jit(solution)/shard_map/transpose(jvp())/while/body/eval_jaxpr/checkpoint/ijx,jc->ixc/dot_general | solution.py:104
  300.2 3.3 copy.79
  311.0 8.7 %fusion.185 = f32[64,64,72]{2,1,0:T(8,128)} fusion(f32[64,64,1]{1,0,2:T(8,128)S(1)} %convolution_bitcast_fusion.4, f32[64,72,64]{2,0,1:T(8,128)S(1)} %bitcast.610), kind=kOutput, calls=%fused_computation.9.clone.1 | convolution fusion | flops 226492416 | bytes 2375680 | tf_op jit(solution)/shard_map/transpose(jvp())/while/body/eval_jaxpr/checkpoint/ijx,jc->ixc/dot_general | solution.py:104
  319.7 3.3 copy.79
  330.5 8.7 %fusion.185 = f32[64,64,72]{2,1,0:T(8,128)} fusion(f32[64,64,1]{1,0,2:T(8,128)S(1)} %convolution_bitcast_fusion.4, f32[64,72,64]{2,0,1:T(8,128)S(1)} %bitcast.610), kind=kOutput, calls=%fused_computation.9.clone.1 | convolution fusion | flops 226492416 | bytes 2375680 | tf_op jit(solution)/shard_map/transpose(jvp())/while/body/eval_jaxpr/checkpoint/ijx,jc->ixc/dot_general | solution.py:104
  339.1 3.3 copy.79
  346.9 1.9 collective-permute-start.9
  348.9 2.4 collective-permute-start.8
  351.3 9.5 %collective-permute-done.8 = f32[1,3,3,3,256]{4,3,2,1,0:T(4,128)S(1)} collective-permute-done((f32[1,3,3,3,256]{4,3,2,1,0:T(4,128)S(1)}, f32[1,3,3,3,256]{4,3,2,1,0:T(4,128)S(1)}, u32[]{:S(2)}, u32[]{:S(2)}) %collective-permute-start.8) | collective-permute-done | bytes 27680 | tf_op jit(solution)/shard_map/ppermute | solution.py:32
  360.8 7.0 %collective-permute-start.11 = (f32[5,1,3,3,256]{4,3,2,1,0:T(4,128)S(1)}, f32[5,1,3,3,256]{4,3,2,1,0:T(4,128)S(1)}, u32[]{:S(2)}, u32[]{:S(2)}) collective-permute-start(f32[5,1,3,3,256]{4,3,2,1,0:T(4,128)S(1)} %get-tuple-element.669), channel_id=1, source_target_pairs={{8,0},{16,8},{24,16},{32,24},{40,32},{48,40},{56,48},{0,56},{9,1},... | collective-permute-start | bytes 138248 | tf_op jit(solution)/shard_map/ppermute | solution.py:34
  367.8 1.9 collective-permute-start.10
  371.2 2.7 collective-permute-done.10
  374.0 6.6 %collective-permute-start.13 = (f32[5,5,1,3,256]{4,3,2,1,0:T(4,128)S(1)}, f32[5,5,1,3,256]{4,3,2,1,0:T(4,128)S(1)}, u32[]{:S(2)}, u32[]{:S(2)}) collective-permute-start(f32[5,5,1,3,256]{4,3,2,1,0:T(4,128)S(1)} %get-tuple-element.664), channel_id=1, source_target_pairs={{1,0},{2,1},{3,2},{4,3},{5,4},{6,5},{7,6},{0,7},{9,8},{10,9},{11,1... | collective-permute-start | bytes 230408 | tf_op jit(solution)/shard_map/ppermute | solution.py:34
  380.6 7.9 %collective-permute-start.12 = (f32[5,5,1,3,256]{4,3,2,1,0:T(4,128)S(1)}, f32[5,5,1,3,256]{4,3,2,1,0:T(4,128)S(1)}, u32[]{:S(2)}, u32[]{:S(2)}) collective-permute-start(f32[5,5,1,3,256]{4,3,2,1,0:T(4,128)S(1)} %get-tuple-element.663), channel_id=1, source_target_pairs={{0,1},{1,2},{2,3},{3,4},{4,5},{5,6},{6,7},{7,0},{8,9},{9,10},{10,1... | collective-permute-start | bytes 230408 | tf_op jit(solution)/shard_map/ppermute | solution.py:32
  389.2 8.8 %collective-permute-done.12 = f32[5,5,1,3,256]{4,3,2,1,0:T(4,128)S(1)} collective-permute-done((f32[5,5,1,3,256]{4,3,2,1,0:T(4,128)S(1)}, f32[5,5,1,3,256]{4,3,2,1,0:T(4,128)S(1)}, u32[]{:S(2)}, u32[]{:S(2)}) %collective-permute-start.12) | collective-permute-done | bytes 76832 | tf_op jit(solution)/shard_map/ppermute | solution.py:32
  (567 shorter events, 105.9 us)
Async XLA Ops:
  0.6 186.8 %copy-start = (bf16[512,512]{1,0:T(8,128)(2,1)S(1)}, bf16[512,512]{1,0:T(8,128)(2,1)}, u32[]{:S(2)}) copy-start(bf16[512,512]{1,0:T(8,128)(2,1)} %param.28) | copy-start | bytes 1572868
  4.4 19.9 %collective-permute-start.1 = (f32[4,64]{1,0:T(4,128)S(1)}, f32[4,64]{1,0:T(4,128)S(1)}, u32[]{:S(2)}, u32[]{:S(2)}) collective-permute-start(f32[4,64]{1,0:T(4,128)S(1)} %get-tuple-element.673), channel_id=1, source_target_pairs={{0,960},{64,0},{128,64},{192,128},{256,192},{320,256},{384,320},{4... | collective-permute-start | bytes 3080 | tf_op jit(solution)/shard_map/ppermute | solution.py:22
  20.2 11.5 %collective-permute-start = (f32[4,64]{1,0:T(4,128)S(1)}, f32[4,64]{1,0:T(4,128)S(1)}, u32[]{:S(2)}, u32[]{:S(2)}) collective-permute-start(f32[4,64]{1,0:T(4,128)S(1)} %get-tuple-element.672), channel_id=1, source_target_pairs={{0,64},{64,128},{128,192},{192,256},{256,320},{320,384},{384,448},... | collective-permute-start | bytes 3080 | tf_op jit(solution)/shard_map/ppermute | solution.py:22
  31.9 4.8 %collective-permute-start.3 = (f32[1,1,1,4,256]{4,3,2,1,0:T(4,128)S(1)}, f32[1,1,1,4,256]{4,3,2,1,0:T(4,128)S(1)}, u32[]{:S(2)}, u32[]{:S(2)}) collective-permute-start(f32[1,1,1,4,256]{4,3,2,1,0:T(4,128)S(1)} %maximum_bitcast_fusion), channel_id=1, source_target_pairs={{64,0},{128,64},{192,128},{256,192},{320,256},{384,320},{448,384},... | collective-permute-start | bytes 12296 | tf_op jit(solution)/shard_map/ppermute | solution.py:34
  34.7 11.5 %collective-permute-start.2 = (f32[1,1,1,4,256]{4,3,2,1,0:T(4,128)S(1)}, f32[1,1,1,4,256]{4,3,2,1,0:T(4,128)S(1)}, u32[]{:S(2)}, u32[]{:S(2)}) collective-permute-start(f32[1,1,1,4,256]{4,3,2,1,0:T(4,128)S(1)} %maximum_bitcast_fusion), channel_id=1, source_target_pairs={{0,64},{64,128},{128,192},{192,256},{256,320},{320,384},{384,448},... | collective-permute-start | bytes 12296 | tf_op jit(solution)/shard_map/ppermute | solution.py:32
  46.3 5.9 %collective-permute-start.5 = (f32[3,1,1,4,256]{4,3,2,1,0:T(4,128)S(1)}, f32[3,1,1,4,256]{4,3,2,1,0:T(4,128)S(1)}, u32[]{:S(2)}, u32[]{:S(2)}) collective-permute-start(f32[3,1,1,4,256]{4,3,2,1,0:T(4,128)S(1)} %pad_maximum_fusion.17), channel_id=1, source_target_pairs={{8,0},{16,8},{24,16},{32,24},{40,32},{48,40},{56,48},{0,56},{9,1},... | collective-permute-start | bytes 36872 | tf_op jit(solution)/shard_map/ppermute | solution.py:34
  48.6 7.0 %collective-permute-start.4 = (f32[3,1,1,4,256]{4,3,2,1,0:T(4,128)S(1)}, f32[3,1,1,4,256]{4,3,2,1,0:T(4,128)S(1)}, u32[]{:S(2)}, u32[]{:S(2)}) collective-permute-start(f32[3,1,1,4,256]{4,3,2,1,0:T(4,128)S(1)} %pad_maximum_fusion.17), channel_id=1, source_target_pairs={{0,8},{8,16},{16,24},{24,32},{32,40},{40,48},{48,56},{56,0},{1,9},... | collective-permute-start | bytes 36872 | tf_op jit(solution)/shard_map/ppermute | solution.py:32
  55.7 17.1 %collective-permute-start.6 = (f32[3,3,1,4,256]{4,3,2,1,0:T(4,128)S(1)}, f32[3,3,1,4,256]{4,3,2,1,0:T(4,128)S(1)}, u32[]{:S(2)}, u32[]{:S(2)}) collective-permute-start(f32[3,3,1,4,256]{4,3,2,1,0:T(4,128)S(1)} %pad_maximum_fusion.15), channel_id=1, source_target_pairs={{0,1},{1,2},{2,3},{3,4},{4,5},{5,6},{6,7},{7,0},{8,9},{9,10},{10,1... | collective-permute-start | bytes 110600 | tf_op jit(solution)/shard_map/ppermute | solution.py:32
  67.6 14.6 %collective-permute-start.7 = (f32[3,3,1,4,256]{4,3,2,1,0:T(4,128)S(1)}, f32[3,3,1,4,256]{4,3,2,1,0:T(4,128)S(1)}, u32[]{:S(2)}, u32[]{:S(2)}) collective-permute-start(f32[3,3,1,4,256]{4,3,2,1,0:T(4,128)S(1)} %pad_maximum_fusion.15), channel_id=1, source_target_pairs={{1,0},{2,1},{3,2},{4,3},{5,4},{6,5},{7,6},{0,7},{9,8},{10,9},{11,1... | collective-permute-start | bytes 110600 | tf_op jit(solution)/shard_map/ppermute | solution.py:34
  183.4 3.5 copy-start.3
  183.4 3.8 copy-start.1
  186.8 1.0 copy-start.4
  187.8 0.8 copy-start.5
  188.7 2.1 copy-start.2
  346.9 4.3 %collective-permute-start.9 = (f32[1,3,3,3,256]{4,3,2,1,0:T(4,128)S(1)}, f32[1,3,3,3,256]{4,3,2,1,0:T(4,128)S(1)}, u32[]{:S(2)}, u32[]{:S(2)}) collective-permute-start(f32[1,3,3,3,256]{4,3,2,1,0:T(4,128)S(1)} %get-tuple-element.671), channel_id=1, source_target_pairs={{64,0},{128,64},{192,128},{256,192},{320,256},{384,320},{448,384},... | collective-permute-start | bytes 82952 | tf_op jit(solution)/shard_map/ppermute | solution.py:34
  348.9 11.9 %collective-permute-start.8 = (f32[1,3,3,3,256]{4,3,2,1,0:T(4,128)S(1)}, f32[1,3,3,3,256]{4,3,2,1,0:T(4,128)S(1)}, u32[]{:S(2)}, u32[]{:S(2)}) collective-permute-start(f32[1,3,3,3,256]{4,3,2,1,0:T(4,128)S(1)} %get-tuple-element.670), channel_id=1, source_target_pairs={{0,64},{64,128},{128,192},{192,256},{256,320},{320,384},{384,448},... | collective-permute-start | bytes 82952 | tf_op jit(solution)/shard_map/ppermute | solution.py:32
  360.8 10.4 %collective-permute-start.11 = (f32[5,1,3,3,256]{4,3,2,1,0:T(4,128)S(1)}, f32[5,1,3,3,256]{4,3,2,1,0:T(4,128)S(1)}, u32[]{:S(2)}, u32[]{:S(2)}) collective-permute-start(f32[5,1,3,3,256]{4,3,2,1,0:T(4,128)S(1)} %get-tuple-element.669), channel_id=1, source_target_pairs={{8,0},{16,8},{24,16},{32,24},{40,32},{48,40},{56,48},{0,56},{9,1},... | collective-permute-start | bytes 138248 | tf_op jit(solution)/shard_map/ppermute | solution.py:34
  367.8 6.1 %collective-permute-start.10 = (f32[5,1,3,3,256]{4,3,2,1,0:T(4,128)S(1)}, f32[5,1,3,3,256]{4,3,2,1,0:T(4,128)S(1)}, u32[]{:S(2)}, u32[]{:S(2)}) collective-permute-start(f32[5,1,3,3,256]{4,3,2,1,0:T(4,128)S(1)} %get-tuple-element.668), channel_id=1, source_target_pairs={{0,8},{8,16},{16,24},{24,32},{32,40},{40,48},{48,56},{56,0},{1,9},... | collective-permute-start | bytes 138248 | tf_op jit(solution)/shard_map/ppermute | solution.py:32
  374.0 15.3 %collective-permute-start.13 = (f32[5,5,1,3,256]{4,3,2,1,0:T(4,128)S(1)}, f32[5,5,1,3,256]{4,3,2,1,0:T(4,128)S(1)}, u32[]{:S(2)}, u32[]{:S(2)}) collective-permute-start(f32[5,5,1,3,256]{4,3,2,1,0:T(4,128)S(1)} %get-tuple-element.664), channel_id=1, source_target_pairs={{1,0},{2,1},{3,2},{4,3},{5,4},{6,5},{7,6},{0,7},{9,8},{10,9},{11,1... | collective-permute-start | bytes 230408 | tf_op jit(solution)/shard_map/ppermute | solution.py:34
  380.6 17.4 %collective-permute-start.12 = (f32[5,5,1,3,256]{4,3,2,1,0:T(4,128)S(1)}, f32[5,5,1,3,256]{4,3,2,1,0:T(4,128)S(1)}, u32[]{:S(2)}, u32[]{:S(2)}) collective-permute-start(f32[5,5,1,3,256]{4,3,2,1,0:T(4,128)S(1)} %get-tuple-element.663), channel_id=1, source_target_pairs={{0,1},{1,2},{2,3},{3,4},{4,5},{5,6},{6,7},{7,0},{8,9},{9,10},{10,1... | collective-permute-start | bytes 230408 | tf_op jit(solution)/shard_map/ppermute | solution.py:32
where the time goes:
time: 401 us; the launch traced here: 399 us
  matrix products  103 us (26%)
  starting transfers between devices  72.8 us (18%)
  local copies, waits for them, and re-layouts  68.4 us (17%)
  other arithmetic  54.4 us (14%)
  waiting for transfers between devices  51 us (13%)
  loops' own time  48.6 us (12%)
    dot_general x16, matrix products, tile_environment(): jnp.einsum('ijx,jc->ixc', mixed, neighbour_embed, precision=lax.Precision...  90.8 us
    another operation x2, loops' own time, local_energy(): lax.scan(visit, start_env, (pair_rows, jnp.arange(pair_rows.shape[0])))  48.6 us
    ppermute x6, waiting for transfers between devices, with_halo(): lax.ppermute(tail, axis, [(i, (i + 1) % count) for i in range(count)])  34.1 us
    ppermute x6, starting transfers between devices, with_halo(): lax.ppermute(tail, axis, [(i, (i + 1) % count) for i in range(count)])  29.5 us
    transpose x8, local copies, waits for them, and re-layouts, tile_environment(): jnp.einsum('ijx,jc->ixc', mixed, neighbour_embed, precision=lax.Precision...  26.7 us
    ppermute x6, starting transfers between devices, with_halo(): lax.ppermute(head, axis, [((i + 1) % count, i) for i in range(count)])  25.6 us
    dynamic_slice x40, local copies, waits for them, and re-layouts, local_energy(): lax.scan(visit, start_env, (pair_rows, jnp.arange(pair_rows.shape[0])))  25.5 us
    ppermute x2, starting transfers between devices, from_behind(): return lax.ppermute(value, axis, pairs)  17.7 us
  transfers between devices with their start and end apart: 14, of which 8 were waited for; matrix products, arithmetic and copies ran while one was open for 1% of the time, Pallas kernels for 0%

commit v1 on v0

v1 whole, which is shorter than its diff:
```python
import functools

import jax
import jax.numpy as jnp
from jax import lax
from jax.experimental import pallas as pl
from jax.experimental.pallas import tpu as pltpu
from jax.sharding import PartitionSpec as P

TILE = 64
NB = 8
PAIRS = 8
SPECIES = 8
CHANNELS = 64
HARM = 9
EDGE = PAIRS * TILE
HALF = EDGE // 2

cell = 10.0
cutoff = 5.0
cutoff_sq = 25.0
soften = 0.25
sharpness = 1.0
env_scale = 0.5

MESH = pl.DeviceIdType.MESH
F32 = jnp.float32
BF16 = jnp.bfloat16

PLANE_FAR = [(a, b) for a in (-2, -1, 0, 1, 2) for b in (-1, 0, 1)]

E_UX, E_UY, E_UZ, E_D, E_INV, E_F, E_SLOPE = range(NB, NB + 7)


def slot_far(a, b):
    return (a + 2) * 3 + (b + 1)


def block_of(a, b, c):
    return (a + 1) * 9 + (b + 1) * 3 + (c + 1)


def iota(shape, dim):
    return lax.broadcasted_iota(jnp.int32, shape, dim)


def three_parts(value):
    high = value.astype(BF16)
    rest = value - high.astype(F32)
    middle = rest.astype(BF16)
    low = (rest - middle.astype(F32)).astype(BF16)
    return high, middle, low


def pick(hot, value, dims):
    total = None
    for part in three_parts(value):
        term = lax.dot_general(hot, part, (dims, ((), ())), preferred_element_type=F32)
        total = term if total is None else total + term
    return total


def contract(left, right, dims):
    return lax.dot_general(left, right, (dims, ((), ())), preferred_element_type=F32)


def kernel(
    sizes,
    pos_hbm,
    kind_hbm,
    list_hbm,
    sent_hbm,
    pair_hbm,
    total_hbm,
    radial_hbm,
    emb_hbm,
    out_hbm,
    first_hbm,
    second_hbm,
    force_ref,
    pos_ref,
    kind_ref,
    list_ref,
    sent_ref,
    pair_ref,
    total_ref,
    radial_ref,
    emb_ref,
    out_ref,
    packed,
    raw,
    rim_out,
    rim_in,
    plane,
    asked_own,
    asked,
    tiles_out,
    tiles_in,
    back_out,
    back_in,
    w_first,
    w_second,
    mix,
    terms,
    back_terms,
    edges,
    centre_at,
    env,
    env_grad,
    features,
    hidden,
    slope,
    pull,
    push,
    send_sem,
    recv_sem,
    load_sem,
):
    here = {axis: lax.axis_index(axis) for axis in ("gx", "gy", "gz")}

    def at(a, b, c):
        return {
            axis: lax.rem(here[axis] + (step + sizes[axis]), sizes[axis])
            for axis, step in (("gx", a), ("gy", b), ("gz", c))
        }

    far = [where for where in PLANE_FAR if where != (0, 0)]
    around = [(a, b, c) for c in (-1, 1, 0) for a in (-1, 0, 1) for b in (-1, 0, 1)]
    around.remove((0, 0, 0))

    barrier = pltpu.get_barrier_semaphore()
    for c in (-1, 1):
        pl.semaphore_signal(barrier, inc=1, device_id=at(0, 0, c), device_id_type=MESH)
    for a, b in far:
        pl.semaphore_signal(barrier, inc=1, device_id=at(a, b, 0), device_id_type=MESH)

    loads = []
    for src, dst in (
        (list_hbm, list_ref),
        (pos_hbm, pos_ref),
        (kind_hbm, kind_ref),
        (sent_hbm, sent_ref),
        (pair_hbm, pair_ref),
        (total_hbm, total_ref),
        (emb_hbm, emb_ref),
        (radial_hbm, radial_ref),
        (first_hbm, w_first),
        (second_hbm, w_second),
        (out_hbm, out_ref),
    ):
        copy = pltpu.make_async_copy(src, dst, load_sem.at[len(loads)])
        copy.start()
        loads.append(copy)
    load_emb, load_radial, load_first, load_second, load_out = loads[6:]
    plane[...] = jnp.zeros(plane.shape, F32)
    for copy in loads[:6]:
        copy.wait()

    counter = [0]

    def remote(src, dst, where, landing):
        index = counter[0]
        counter[0] += 1
        return pltpu.make_async_remote_copy(
            src_ref=src,
            dst_ref=dst,
            send_sem=send_sem.at[index],
            recv_sem=recv_sem.at[landing],
            device_id=at(*where),
            device_id_type=MESH,
        )

    lane = iota((1, 2 * TILE), 1)
    left_half = lane < TILE
    sub = iota((8, 2 * TILE), 0)

    def swap(value):
        return pltpu.roll(value, TILE, axis=value.ndim - 1)

    packed[0:1, :] = pos_ref[0]
    packed[1:2, :] = pos_ref[1]
    packed[2:3, :] = pos_ref[2]
    packed[3:4, :] = kind_ref[...].astype(F32)
    packed[4:8, :] = jnp.zeros((4, 2 * TILE), F32)
    atoms = packed[...]
    lists = list_ref[...]
    named = jnp.concatenate([lists[1:2], lists[0:1]], axis=1)
    live_lanes = jnp.where(left_half, sent_ref[0, 1], sent_ref[0, 0] + TILE)
    live = (lane < live_lanes).astype(F32)
    hot = (iota((2 * TILE, 2 * TILE), 0) == named).astype(F32).astype(BF16)
    leaving = contract(
        jnp.broadcast_to(live, (16, 2 * TILE)).astype(BF16), hot, ((1,), (1,))
    )[0:8]
    stacked = jnp.concatenate([part.astype(F32) for part in three_parts(atoms)], axis=0)
    stacked = jnp.concatenate([stacked, jnp.zeros((8, 2 * TILE), F32)], axis=0).astype(BF16)
    moved = contract(stacked, hot, ((1,), (0,)))
    moved = moved[0:8] + moved[8:16] + moved[16:24]
    moved = jnp.where((sub == 3) & (live < 0.5), -1.0, moved)
    staying = jnp.where((sub == 3) & (leaving > 0.5), -1.0, atoms)
    own = slot_far(0, 0)
    moved_swap = swap(moved)
    staying_swap = swap(staying)

    def put_row(row, one, other):
        raw[own, row : row + 1, 0:128] = jnp.where(left_half, one[0:1], other[1:2])
        raw[own, row : row + 1, 128:256] = jnp.where(left_half, one[2:3], other[3:4])

    put_row(0, moved, moved_swap)
    put_row(1, staying, staying_swap)
    put_row(2, staying_swap, staying)
    put_row(3, moved_swap, moved)
    rim_out[0] = raw[own, 0:1, :]
    rim_out[1] = raw[own, 3:4, :]

    pair_total = total_ref[0, 0, 0]
    want = jnp.full((8, 128), -1, jnp.int32)
    want_centre = jnp.full((8, 128), -1, jnp.int32)
    level = jnp.zeros((8, 128), jnp.int32)
    centres = []
    for p in range(PAIRS):
        active = p < pair_total
        centre = jnp.where(active, pair_ref[0, p], -1)
        other = jnp.where(active, pair_ref[1, p], -1)
        centres.append(centre)
        want = jnp.where(sub == p, other, want)
        want_centre = jnp.where(sub == p, jnp.where(active, centre + 13 * 4, -1), want_centre)
        level = jnp.where(sub == p, lax.rem(lax.div(other + 12, 4), 3) - 1, level)
    want = want.astype(F32)
    want_centre = want_centre.astype(F32)
    asked_own[...] = want

    pl.semaphore_wait(barrier, len(far) + 2)

    ask = [
        remote(asked_own, asked.at[1], (0, 0, -1), 0),
        remote(asked_own, asked.at[0], (0, 0, 1), 1),
    ]
    for copy in ask:
        copy.start()
    ghosts = []
    rims = []
    for a, b in sorted(far, key=lambda where: -abs(where[0])):
        landing = slot_far(-a, -b)
        if abs(a) == 2:
            side = 0 if a > 0 else 1
            place = side * 3 + (1 - b)
            copy = remote(rim_out.at[side], rim_in.at[place], (a, b, 0), 2 + landing)
            rims.append((copy, place, side, -a, -b))
        else:
            copy = remote(raw.at[own], raw.at[landing], (a, b, 0), 2 + landing)
            ghosts.append((copy, -a, -b))
        copy.start()

    load_emb.wait()
    load_radial.wait()
    wide = iota((1, 4 * TILE), 1)
    tile_of_lane = lax.shift_right_logical(wide, 6)
    emb = emb_ref[...]
    emb_twice = jnp.concatenate([emb, emb], axis=1)
    radial_twice = jnp.concatenate([radial_ref[...], radial_ref[...]], axis=1)
    emb_wide = jnp.concatenate([emb_twice, emb_twice], axis=1) * env_scale
    radial_wide = jnp.concatenate([radial_twice, radial_twice], axis=1)
    chosen = [(tile_of_lane == centres[p]).astype(F32) for p in range(PAIRS)]
    table = []
    for n in range(NB):
        base = emb_wide * radial_wide[n : n + 1]
        table.append(
            jnp.concatenate([base * chosen[p] for p in range(PAIRS)], axis=0).astype(BF16)
        )

    edge_lane = iota((8, EDGE), 1)
    edge_pair = lax.shift_right_logical(edge_lane, 6)
    pair_mask = edge_pair == iota((8, EDGE), 0)
    pair_hot = pair_mask.astype(F32)

    wide_xy = lax.shift_right_logical(wide, 6)

    def shifted(a, b):
        return jnp.where(wide_xy == 0, a * cell, 0.0) + jnp.where(wide_xy == 1, b * cell, 0.0)

    plane[4 * own : 4 * own + 4, :] = raw[own]
    for copy, a, b in ghosts:
        copy.wait_recv()
        k = slot_far(a, b)
        plane[4 * k : 4 * k + 4, :] = raw[k] + shifted(float(a), float(b))
    for copy, place, side, a, b in rims:
        copy.wait_recv()
        k = 4 * slot_far(a, b) + 3 * side
        plane[k : k + 1, :] = rim_in[place] + shifted(float(a), float(b))
    for copy in ask:
        copy.wait_recv()

    row = iota((1, 64), 1)
    part = jnp.bitwise_and(row, 3)
    block = lax.shift_right_logical(row, 2)
    far_x = lax.shift_right_logical(block * 11, 5)
    far_y = block - far_x * 3
    near_x = far_x - 1 + (part == 0).astype(jnp.int32) - (part == 3).astype(jnp.int32)
    raw_ok = (near_x >= 0) & (near_x <= 2) & (block < 15)
    raw_base = jnp.where(raw_ok, (9 * near_x + 3 * far_y) * 4 + part, -100)

    def asked_rows(base, parts):
        return jnp.concatenate(
            [
                (values[:, :64] == (base + 4 * (c + 1)).astype(F32)).astype(F32)
                for values, c in parts
            ],
            axis=0,
        ).astype(BF16)

    lower = asked[0]
    upper = asked[1]
    which = asked_rows(raw_base, [(want, 0), (lower, 1), (upper, -1), (want_centre, 0)])
    picked = pick(which, plane[...], ((1,), (0,)))
    tiles_out[0] = picked[8:16]
    tiles_out[1] = picked[16:24]
    fetch = [
        remote(tiles_out.at[0], tiles_in.at[1], (0, 0, -1), 17),
        remote(tiles_out.at[1], tiles_in.at[0], (0, 0, 1), 18),
    ]
    for copy in fetch:
        copy.start()

    pair_hot16 = pair_hot.astype(BF16)
    spread = None
    for piece in three_parts(picked[24:32]):
        term = contract(piece, pair_hot16, ((0,), (0,)))
        spread = term if spread is None else spread + term
    centre_at[...] = spread

    tile_rows = [
        plane[4 * slot_far(-1, 0) : 4 * slot_far(-1, 0) + 1, 128:256],
        plane[4 * own + 1 : 4 * own + 2, 128:256],
        plane[4 * own + 2 : 4 * own + 3, 128:256],
        plane[4 * slot_far(1, 0) + 3 : 4 * slot_far(1, 0) + 4, 128:256],
    ]
    kinds = jnp.concatenate(
        [
            jnp.where(left_half, swap(tile_rows[0]), tile_rows[1]),
            jnp.where(left_half, swap(tile_rows[2]), tile_rows[3]),
        ],
        axis=1,
    )
    kind_hot = (kinds == iota((SPECIES, 256), 0).astype(F32)).astype(F32).astype(BF16)
    centre_emb = contract(kind_hot, emb_twice.astype(BF16), ((0,), (0,)))

    def pair_row(values):
        tiled = jnp.concatenate([values] * 4, axis=1)
        return jnp.sum(jnp.where(pair_mask, tiled, 0.0), axis=0, keepdims=True)

    same = pair_row((want == want_centre).astype(F32))
    centre_row = jnp.zeros((1, EDGE), jnp.int32) - 1
    for p in range(PAIRS):
        centre_row = jnp.where(edge_pair[0:1] == p, centres[p], centre_row)
    centre_hot = (centre_row == iota((16, EDGE), 0)).astype(F32).astype(BF16)
    lane_j = jnp.bitwise_and(edge_lane[0:1], TILE - 1)

    for copy in fetch:
        copy.wait_recv()
    lift = jnp.where(left_half, level.astype(F32) * cell, 0.0)
    others = picked[0:8] + tiles_in[0] + tiles_in[1]
    xy = others[:, :128]
    zs = others[:, 128:256] + lift
    xy_swap = swap(xy)
    zs_swap = swap(zs)
    other_x = pair_row(jnp.where(left_half, xy, xy_swap))
    other_y = pair_row(jnp.where(left_half, xy_swap, xy))
    other_z = pair_row(jnp.where(left_half, zs, zs_swap))
    other_kind = pair_row(jnp.where(left_half, zs_swap, zs))
    other_live = (other_kind >= 0).astype(F32)

    kind_rows = iota((SPECIES, EDGE), 0).astype(F32)
    of_kind = (other_kind == kind_rows).astype(F32)
    other_hot = jnp.concatenate(
        [of_kind * (edge_pair == p).astype(F32) for p in range(PAIRS)], axis=0
    ).astype(BF16)
    for n in range(NB):
        mix[n * EDGE : (n + 1) * EDGE, :] = contract(
            other_hot, table[n], ((0,), (0,))
        ).astype(BF16)

    spots = [cutoff * (n + 1) / NB for n in range(NB)]

    def forward(step, carry):
        start = pl.multiple_of(step * 16, 16)
        rows = pl.ds(start, 16)
        row_i = iota((16, HALF), 0) + start
        for g in range(2):
            cols = slice(g * HALF, (g + 1) * HALF)
            dx = other_x[:, cols] - centre_at[pl.ds(start, 16), cols]
            dy = other_y[:, cols] - centre_at[pl.ds(start + TILE, 16), cols]
            dz = other_z[:, cols] - centre_at[pl.ds(start + 2 * TILE, 16), cols]
            kind_i = centre_at[pl.ds(start + 3 * TILE, 16), cols]
            squared = dx * dx + dy * dy + dz * dz
            inverse = lax.rsqrt(squared + soften)
            distance = (squared + soften) * inverse
            keep = jnp.where(kind_i >= 0, other_live[:, cols], 0.0)
            keep = jnp.where((row_i == lane_j[:, cols]) & (same[:, cols] > 0.5), 0.0, keep)
            inside = jnp.maximum(1.0 - squared * (1.0 / cutoff_sq), 0.0)
            slope_f = inside * keep
            envelope = inside * slope_f
            ux = dx * inverse
            uy = dy * inverse
            uz = dz * inverse
            edges[E_UX, rows, cols] = ux
            edges[E_UY, rows, cols] = uy
            edges[E_UZ, rows, cols] = uz
            edges[E_D, rows, cols] = distance
            edges[E_INV, rows, cols] = inverse
            edges[E_F, rows, cols] = envelope
            edges[E_SLOPE, rows, cols] = slope_f
            harmonics = [
                None,
                ux,
                uy,
                uz,
                ux * uy,
                uy * uz,
                1.5 * uz * uz - 0.5,
                ux * uz,
                0.5 * (ux * ux - uy * uy),
            ]
            for n in range(NB):
                away = distance - spots[n]
                bump = jnp.exp(-sharpness * away * away)
                edges[n, rows, cols] = bump
                radial = bump * envelope
                depth = slice(n * EDGE + g * HALF, n * EDGE + (g + 1) * HALF)
                for m in range(HARM):
                    value = radial if m == 0 else radial * harmonics[m]
                    terms[pl.ds(start + m * TILE, 16), depth] = value.astype(BF16)
        return carry

    lax.fori_loop(0, TILE // 16, forward, 0)

    middle_row = HARM * TILE // 2
    env[:middle_row, :] = contract(terms[:middle_row, :], mix[...], ((1,), (0,)))
    env[middle_row:, :] = contract(terms[middle_row:, :], mix[...], ((1,), (0,)))

    def band(first, last):
        total = None
        for m in range(first, last):
            value = env[m * TILE : (m + 1) * TILE, :]
            total = value * value if total is None else total + value * value
        return total

    zeroth = band(0, 1)
    vector = band(1, 4)
    tensor = band(4, 9)
    for t in range(4):
        rows = slice(t * TILE, (t + 1) * TILE)
        cols = slice((t // 2) * 128, (t // 2) * 128 + 128)
        if t % 2 == 0:
            low = jnp.where(left_half, zeroth[:, cols], swap(vector[:, cols]))
            high = jnp.where(left_half, tensor[:, cols], centre_emb[rows])
        else:
            low = jnp.where(left_half, swap(zeroth[:, cols]), vector[:, cols])
            high = jnp.where(left_half, swap(tensor[:, cols]), centre_emb[rows])
        features[rows, 0:128] = low.astype(BF16)
        features[rows, 128:256] = high.astype(BF16)

    load_first.wait()
    before = contract(features[...], w_first[...], ((1,), (0,)))
    gate = 0.5 + 0.5 * jnp.tanh(0.5 * before)
    value = before * gate
    hidden[...] = value.astype(BF16)
    slope[...] = gate + value * (1.0 - gate)
    load_second.wait()
    before = contract(hidden[...], w_second[...], ((1,), (0,)))
    gate = 0.5 + 0.5 * jnp.tanh(0.5 * before)
    value = before * gate
    hidden[...] = value.astype(BF16)

    load_out.wait()
    w_out_parts = [part.astype(F32) for part in three_parts(out_ref[...])]
    turn = ((gate + value * (1.0 - gate)) * w_out_parts[0]).astype(BF16)
    turn = contract(turn, w_second[...], ((1,), (1,)))
    turn = (turn * slope[...]).astype(BF16)
    turn = contract(turn, w_first[...], ((1,), (1,)))
    for h in range(2):
        even = turn[2 * h * TILE : (2 * h + 1) * TILE]
        odd = turn[(2 * h + 1) * TILE : (2 * h + 2) * TILE]
        cols = slice(h * 128, (h + 1) * 128)
        pulls = [
            2.0 * jnp.where(left_half, even[:, 0:128], swap(odd[:, 0:128])),
            2.0 * jnp.where(left_half, swap(even[:, 0:128]), odd[:, 0:128]),
            2.0 * jnp.where(left_half, even[:, 128:256], swap(odd[:, 128:256])),
        ]
        for m in range(HARM):
            rows = slice(m * TILE, (m + 1) * TILE)
            kind = 0 if m == 0 else (1 if m < 4 else 2)
            env_grad[rows, cols] = (env[rows, cols] * pulls[kind]).astype(BF16)

    back_terms[...] = contract(env_grad[...], mix[...], ((1,), (1,)))

    push[...] = jnp.zeros(push.shape, F32)
    pull[3 * TILE :, :] = jnp.zeros((TILE, EDGE), F32)

    def backward(step, carry):
        start = pl.multiple_of(step * 8, 8)
        rows = pl.ds(start, 8)
        for g in range(2):
            cols = slice(g * HALF, (g + 1) * HALF)
            ux = edges[E_UX, rows, cols]
            uy = edges[E_UY, rows, cols]
            uz = edges[E_UZ, rows, cols]
            distance = edges[E_D, rows, cols]
            inverse = edges[E_INV, rows, cols]
            envelope = edges[E_F, rows, cols]
            harmonics = [
                None,
                ux,
                uy,
                uz,
                ux * uy,
                uy * uz,
                1.5 * uz * uz - 0.5,
                ux * uz,
                0.5 * (ux * ux - uy * uy),
            ]
            turned = [None] * HARM
            plain = None
            spotted = None
            for n in range(NB):
                bump = edges[n, rows, cols]
                depth = slice(n * EDGE + g * HALF, n * EDGE + (g + 1) * HALF)
                along = None
                for m in range(HARM):
                    value = back_terms[pl.ds(start + m * TILE, 8), depth]
                    if m == 0:
                        along = value
                    else:
                        along = along + value * harmonics[m]
                        piece = value * bump
                        turned[m] = piece if n == 0 else turned[m] + piece
                along = along * bump
                plain = along if n == 0 else plain + along
                spotted = along * spots[n] if n == 0 else spotted + along * spots[n]
            to_x = turned[1] + turned[4] * uy + turned[7] * uz + turned[8] * ux
            to_y = turned[2] + turned[4] * ux + turned[5] * uz - turned[8] * uy
            to_z = turned[3] + turned[5] * uy + 3.0 * turned[6] * uz + turned[7] * ux
            scaled = envelope * inverse
            by_d = -2.0 * sharpness * (distance * plain - spotted) * envelope
            by_d = by_d - (to_x * ux + to_y * uy + to_z * uz) * scaled
            by_q = -2.0 / cutoff_sq * plain * edges[E_SLOPE, rows, cols]
            radial = by_d + 2.0 * distance * by_q
            for axis, to, unit in ((0, to_x, ux), (1, to_y, uy), (2, to_z, uz)):
                flow = to * scaled + unit * radial
                pull[pl.ds(start + axis * TILE, 8), cols] = flow
                push[axis, :, cols] = push[axis, :, cols] + flow
        return carry

    lax.fori_loop(0, TILE // 8, backward, 0)

    folded = []
    for axis in range(3):
        total = jnp.sum(push[axis], axis=0, keepdims=True)
        spread_out = jnp.where(pair_mask, total, 0.0)
        narrow = (
            spread_out[:, 0:128]
            + spread_out[:, 128:256]
            + spread_out[:, 256:384]
            + spread_out[:, 384:512]
        )
        folded.append(narrow + swap(narrow))
    grads = jnp.concatenate(
        [
            jnp.where(left_half, folded[0], folded[1]),
            jnp.where(left_half, folded[2], 0.0),
            jnp.where(left_half, 0.0, folded[2]),
        ],
        axis=0,
    )
    message_row = iota((1, 256), 1)
    message_part = jnp.bitwise_and(message_row, 7)
    message_base = lax.shift_right_logical(message_row, 3) * 4
    flat = jnp.where(message_part < 4, message_base + message_part, -100)
    deep = jnp.where(
        (message_part == 4) | (message_part == 5), message_base + 2 * (message_part - 4), -100
    )
    want_wide = jnp.concatenate([want, want], axis=1)
    owner = jnp.concatenate(
        [(want_wide == rows.astype(F32)).astype(F32) for rows in (flat, deep, deep + 1)], axis=0
    ).astype(BF16)
    owed = None
    for piece in three_parts(grads):
        term = contract(owner, piece, ((0,), (0,)))
        owed = term if owed is None else owed + term
    for k in range(27):
        back_out[k] = owed[8 * k : 8 * k + 8]
    returns = []
    for a, b, c in around:
        landing = block_of(-a, -b, -c)
        copy = remote(
            back_out.at[block_of(a, b, c), pl.ds(0, 6)],
            back_in.at[landing, pl.ds(0, 6)],
            (a, b, c),
            19 + landing,
        )
        copy.start()
        returns.append((copy, landing))

    centre_grad = None
    for piece in three_parts(pull[...]):
        term = contract(centre_hot, piece, ((1,), (1,)))
        centre_grad = term if centre_grad is None else centre_grad + term

    w_out_rows = jnp.concatenate(w_out_parts + [jnp.zeros((13, hidden.shape[1]), F32)], axis=0)
    energy = contract(w_out_rows.astype(BF16), hidden[...], ((1,), (1,)))
    energy = energy[0:1] + energy[1:2] + energy[2:3]
    force_ref[3] = jnp.where(kinds >= 0, -energy, 0.0)

    own_block = block_of(0, 0, 0)
    gradient = owed[8 * own_block : 8 * own_block + 6]
    for copy, landing in returns:
        copy.wait_recv()
        gradient = gradient + back_in[landing, 0:6]

    centre_xy = centre_grad[0:4, 0:128]
    centre_z = centre_grad[0:4, 128:256]
    centre_z_swap = swap(centre_z)
    xy = gradient[0:4] - centre_xy
    xy_swap = swap(xy)
    for h in range(2):
        cols = slice(h * 128, (h + 1) * 128)
        even = slice(2 * h, 2 * h + 1)
        odd = slice(2 * h + 1, 2 * h + 2)
        force_ref[0, 0:1, cols] = jnp.where(left_half, xy[even], xy_swap[odd])
        force_ref[1, 0:1, cols] = jnp.where(left_half, xy_swap[even], xy[odd])
        force_ref[2, 0:1, cols] = gradient[4 + h : 5 + h] - jnp.where(
            left_half, centre_z[even], centre_z_swap[odd]
        )

    for copy in ask + fetch:
        copy.wait_send()
    for copy, *_ in ghosts + rims:
        copy.wait_send()
    for copy, _ in returns:
        copy.wait_send()


def local(sizes, positions, species, lists, sent, pairs, total, radial, emb, first, second, out):
    hidden = first.shape[1]
    vmem = pl.BlockSpec(memory_space=pltpu.VMEM)
    anywhere = pl.BlockSpec(memory_space=pltpu.HBM)
    both = pl.pallas_call(
        functools.partial(kernel, sizes),
        out_shape=jax.ShapeDtypeStruct((4, 1, 4 * TILE), F32),
        in_specs=[anywhere] * 11,
        out_specs=vmem,
        scratch_shapes=[
            pltpu.VMEM((3, 1, 128), F32),
            pltpu.VMEM((1, 128), jnp.int32),
            pltpu.VMEM((2, 64), jnp.int32),
            pltpu.SMEM((1, 2), jnp.int32),
            pltpu.SMEM((2, PAIRS), jnp.int32),
            pltpu.SMEM((1, 1, 1), jnp.int32),
            pltpu.VMEM(radial.shape, F32),
            pltpu.VMEM(emb.shape, F32),
            pltpu.VMEM((1, hidden), F32),
            pltpu.VMEM((8, 128), F32),
            pltpu.VMEM((15, 4, 256), F32),
            pltpu.VMEM((2, 1, 256), F32),
            pltpu.VMEM((6, 1, 256), F32),
            pltpu.VMEM((64, 256), F32),
            pltpu.VMEM((8, 128), F32),
            pltpu.VMEM((2, 8, 128), F32),
            pltpu.VMEM((2, 8, 256), F32),
            pltpu.VMEM((2, 8, 256), F32),
            pltpu.VMEM((27, 8, 128), F32),
            pltpu.VMEM((27, 8, 128), F32),
            pltpu.VMEM(first.shape, BF16),
            pltpu.VMEM(second.shape, BF16),
            pltpu.VMEM((NB * EDGE, 256), BF16),
            pltpu.VMEM((HARM * TILE, NB * EDGE), BF16),
            pltpu.VMEM((HARM * TILE, NB * EDGE), F32),
            pltpu.VMEM((NB + 7, TILE, EDGE), F32),
            pltpu.VMEM((4 * TILE, EDGE), F32),
            pltpu.VMEM((HARM * TILE, 256), F32),
            pltpu.VMEM((HARM * TILE, 256), BF16),
            pltpu.VMEM((256, 256), BF16),
            pltpu.VMEM((256, hidden), BF16),
            pltpu.VMEM((256, hidden), F32),
            pltpu.VMEM((4 * TILE, EDGE), F32),
            pltpu.VMEM((3, 8, EDGE), F32),
            pltpu.SemaphoreType.DMA((44,)),
            pltpu.SemaphoreType.DMA((46,)),
            pltpu.SemaphoreType.DMA((11,)),
        ],
        compiler_params=pltpu.CompilerParams(
            collective_id=0, has_side_effects=True, vmem_limit_bytes=56 * 1024 * 1024
        ),
    )(
        positions.reshape(3, 1, 128),
        species.reshape(1, 128),
        lists.reshape(2, 64),
        sent.reshape(1, 2),
        pairs.reshape(PAIRS, 2).T,
        total,
        radial,
        emb,
        out.reshape(1, hidden),
        first,
        second,
    )
    return -both[:3].reshape(1, 1, 1, 3, 4 * TILE), -both[3].reshape(1, 1, 1, 4 * TILE)


def solution(mesh):
    sizes = dict(mesh.shape)
    placed = (
        P("gx", "gy", "gz", None, None),
        P("gx", "gy", "gz", None),
        P("gx", "gy", "gz", None, None),
        P("gx", "gy", "gz", None),
        P("gx", "gy", "gz", None, None),
        P("gx", "gy", "gz"),
        P(),
        P(),
        P(),
        P(),
        P(),
    )
    return jax.shard_map(
        functools.partial(local, sizes),
        mesh=mesh,
        in_specs=placed,
        out_specs=(P("gx", "gy", "gz", None, None), P("gx", "gy", "gz", None)),
        check_vma=False,
    )
```

time: 401 us -> 64.6 us (0.16)
  the two profiles are of different devices: /device:TPU:8 before, /device:TPU:1 now
where the time goes in v1:
time: 64.6 us; the launch traced here: 64.4 us
  Pallas kernels  60.7 us (94%)
  other arithmetic  2.48 us (4%)
  between operations  1.29 us (2%)
    pallas_call x1, Pallas kernels, local(): pl.pallas_call(functools.partial(kernel, sizes), out_shape=jax.ShapeDtype...  60.7 us

profile of v1, /device:TPU:1, one launch (start us, length us, event | category | flops | bytes accessed | tf_op | source)
XLA Modules:
  0.0 64.4 jit_solution(11812131958170454859)
XLA Ops:
  1.3 60.7 %shard_map.122 = f32[4,1,256]{2,1,0:T(1,128)} custom-call(f32[3,1,128]{2,1,0:T(1,128)} %bitcast.15, s32[1,128]{1,0:T(1,128)} %bitcast.18, s32[2,64]{1,0:T(2,128)} %bitcast.16, s32[1,2]{1,0:T(1,128)} %bitcast.19, s32[2,8]{1,0:T(2,128)} %bitcast.17, s32[1,1,1]{2,1,0:T(1,128)S(6)} %copy.14.total_hbm, f32[8,64]{1,0:T(8,128)} %radial_hbm.1, f32[8,64]{1,0:T(8,128)} %emb_hbm.1, ...), custom_call_target="tpu_custom_call" | custom-call | tf_op jit(solution)/shard_map/pallas_call | solution.py:646
  62.0 1.2 %negate_bitcast_fusion.1 = f32[1,1,1,256]{3,2,1,0:T(1,128)} fusion(f32[4,1,256]{2,1,0:T(1,128)} %shard_map.122), kind=kLoop, calls=%fused_computation.1 | loop fusion | flops 256 | bytes 2048 | tf_op jit(solution)/shard_map/neg | solution.py:706
  63.2 1.3 %negate_bitcast_fusion = f32[1,1,1,3,256]{4,2,3,1,0:T(1,128)} fusion(f32[4,1,256]{2,1,0:T(1,128)} %shard_map.122), kind=kLoop, calls=%fused_computation | loop fusion | flops 768 | bytes 6144

commit v2 on v1

--- a/solution.py
+++ b/solution.py
@@ -29,7 +29,7 @@
 
 PLANE_FAR = [(a, b) for a in (-2, -1, 0, 1, 2) for b in (-1, 0, 1)]
 
-E_UX, E_UY, E_UZ, E_D, E_INV, E_F, E_SLOPE = range(NB, NB + 7)
+E_UX, E_UY, E_UZ, E_XY, E_YZ, E_ZZ, E_XZ, E_XX, E_D, E_INV, E_F, E_SLOPE = range(NB, NB + 12)
 
 
 def slot_far(a, b):
@@ -102,7 +102,7 @@
     w_second,
     mix,
     terms,
-    back_terms,
+    turned,
     edges,
     centre_at,
     env,
@@ -409,33 +409,32 @@
             edges[E_INV, rows, cols] = inverse
             edges[E_F, rows, cols] = envelope
             edges[E_SLOPE, rows, cols] = slope_f
-            harmonics = [
-                None,
-                ux,
-                uy,
-                uz,
-                ux * uy,
-                uy * uz,
-                1.5 * uz * uz - 0.5,
-                ux * uz,
-                0.5 * (ux * ux - uy * uy),
-            ]
-            for n in range(NB):
-                away = distance - spots[n]
-                bump = jnp.exp(-sharpness * away * away)
-                edges[n, rows, cols] = bump
-                radial = bump * envelope
-                depth = slice(n * EDGE + g * HALF, n * EDGE + (g + 1) * HALF)
-                for m in range(HARM):
-                    value = radial if m == 0 else radial * harmonics[m]
-                    terms[pl.ds(start + m * TILE, 16), depth] = value.astype(BF16)
+            edges[E_XY, rows, cols] = ux * uy
+            edges[E_YZ, rows, cols] = uy * uz
+            edges[E_ZZ, rows, cols] = 1.5 * uz * uz - 0.5
+            edges[E_XZ, rows, cols] = ux * uz
+            edges[E_XX, rows, cols] = 0.5 * (ux * ux - uy * uy)
         return carry
 
     lax.fori_loop(0, TILE // 16, forward, 0)
 
     middle_row = HARM * TILE // 2
-    env[:middle_row, :] = contract(terms[:middle_row, :], mix[...], ((1,), (0,)))
-    env[middle_row:, :] = contract(terms[middle_row:, :], mix[...], ((1,), (0,)))
+    sums = [None, None]
+    for n in range(NB):
+        away = edges[E_D] - spots[n]
+        bump = jnp.exp(-sharpness * away * away)
+        edges[n] = bump
+        radial = bump * edges[E_F]
+        cols = slice(n * EDGE, (n + 1) * EDGE)
+        for m in range(HARM):
+            value = radial if m == 0 else radial * edges[E_UX + m - 1]
+            terms[m * TILE : (m + 1) * TILE, cols] = value.astype(BF16)
+        for h in range(2):
+            part_rows = slice(h * middle_row, (h + 1) * middle_row)
+            term = contract(terms[part_rows, cols], mix[cols, :], ((1,), (0,)))
+            sums[h] = term if n == 0 else sums[h] + term
+    env[:middle_row, :] = sums[0]
+    env[middle_row:, :] = sums[1]
 
     def band(first, last):
         total = None
@@ -491,7 +490,18 @@
             kind = 0 if m == 0 else (1 if m < 4 else 2)
             env_grad[rows, cols] = (env[rows, cols] * pulls[kind]).astype(BF16)
 
-    back_terms[...] = contract(env_grad[...], mix[...], ((1,), (1,)))
+    for n in range(NB):
+        bump = edges[n]
+        cols = slice(n * EDGE, (n + 1) * EDGE)
+        back = contract(env_grad[...], mix[cols, :], ((1,), (1,)))
+        along = None
+        for m in range(HARM):
+            value = back[m * TILE : (m + 1) * TILE]
+            piece = value * bump
+            turned[m] = piece if n == 0 else turned[m] + piece
+            along = piece if m == 0 else along + piece * edges[E_UX + m - 1]
+        along = along * spots[n]
+        turned[HARM] = along if n == 0 else turned[HARM] + along
 
     push[...] = jnp.zeros(push.shape, F32)
     pull[3 * TILE :, :] = jnp.zeros((TILE, EDGE), F32)
@@ -505,47 +515,21 @@
             uy = edges[E_UY, rows, cols]
             uz = edges[E_UZ, rows, cols]
             distance = edges[E_D, rows, cols]
-            inverse = edges[E_INV, rows, cols]
             envelope = edges[E_F, rows, cols]
-            harmonics = [
-                None,
-                ux,
-                uy,
-                uz,
-                ux * uy,
-                uy * uz,
-                1.5 * uz * uz - 0.5,
-                ux * uz,
-                0.5 * (ux * ux - uy * uy),
-            ]
-            turned = [None] * HARM
-            plain = None
-            spotted = None
-            for n in range(NB):
-                bump = edges[n, rows, cols]
-                depth = slice(n * EDGE + g * HALF, n * EDGE + (g + 1) * HALF)
-                along = None
-                for m in range(HARM):
-                    value = back_terms[pl.ds(start + m * TILE, 8), depth]
-                    if m == 0:
-                        along = value
-                    else:
-                        along = along + value * harmonics[m]
-                        piece = value * bump
-                        turned[m] = piece if n == 0 else turned[m] + piece
-                along = along * bump
-                plain = along if n == 0 else plain + along
-                spotted = along * spots[n] if n == 0 else spotted + along * spots[n]
-            to_x = turned[1] + turned[4] * uy + turned[7] * uz + turned[8] * ux
-            to_y = turned[2] + turned[4] * ux + turned[5] * uz - turned[8] * uy
-            to_z = turned[3] + turned[5] * uy + 3.0 * turned[6] * uz + turned[7] * ux
-            scaled = envelope * inverse
-            by_d = -2.0 * sharpness * (distance * plain - spotted) * envelope
+            to = [turned[m, rows, cols] for m in range(HARM)]
+            plain = to[0]
+            for m in range(1, HARM):
+                plain = plain + to[m] * edges[E_UX + m - 1, rows, cols]
+            to_x = to[1] + to[4] * uy + to[7] * uz + to[8] * ux
+            to_y = to[2] + to[4] * ux + to[5] * uz - to[8] * uy
+            to_z = to[3] + to[5] * uy + 3.0 * to[6] * uz + to[7] * ux
+            scaled = envelope * edges[E_INV, rows, cols]
+            by_d = -2.0 * sharpness * (distance * plain - turned[HARM, rows, cols]) * envelope
             by_d = by_d - (to_x * ux + to_y * uy + to_z * uz) * scaled
             by_q = -2.0 / cutoff_sq * plain * edges[E_SLOPE, rows, cols]
             radial = by_d + 2.0 * distance * by_q
-            for axis, to, unit in ((0, to_x, ux), (1, to_y, uy), (2, to_z, uz)):
-                flow = to * scaled + unit * radial
+            for axis, side, unit in ((0, to_x, ux), (1, to_y, uy), (2, to_z, uz)):
+                flow = side * scaled + unit * radial
                 pull[pl.ds(start + axis * TILE, 8), cols] = flow
                 push[axis, :, cols] = push[axis, :, cols] + flow
         return carry
@@ -673,8 +657,8 @@
             pltpu.VMEM(second.shape, BF16),
             pltpu.VMEM((NB * EDGE, 256), BF16),
             pltpu.VMEM((HARM * TILE, NB * EDGE), BF16),
-            pltpu.VMEM((HARM * TILE, NB * EDGE), F32),
-            pltpu.VMEM((NB + 7, TILE, EDGE), F32),
+            pltpu.VMEM((HARM + 1, TILE, EDGE), F32),
+            pltpu.VMEM((NB + 12, TILE, EDGE), F32),
             pltpu.VMEM((4 * TILE, EDGE), F32),
             pltpu.VMEM((HARM * TILE, 256), F32),
             pltpu.VMEM((HARM * TILE, 256), BF16),

time: 64.6 us -> 62.4 us (0.966)
  Pallas kernels: 60.7 us -> 58.4 us
    pallas_call x1, Pallas kernels: 60.7 us -> 58.4 us  [local(): pl.pallas_call(functools.partial(kernel, sizes), out_shape=jax.ShapeDtype...]
where the time goes in v2:
time: 62.4 us; the launch traced here: 62.2 us
  Pallas kernels  58.4 us (94%)
  other arithmetic  2.48 us (4%)
  between operations  1.29 us (2%)
    pallas_call x1, Pallas kernels, local(): pl.pallas_call(functools.partial(kernel, sizes), out_shape=jax.ShapeDtype...  58.4 us
    unnamed x1, other arithmetic  1.26 us

profile of v2, /device:TPU:1, one launch (start us, length us, event | category | flops | bytes accessed | tf_op | source)
XLA Modules:
  0.0 62.2 jit_solution(15110831713166587494)
XLA Ops:
  1.3 58.4 %shard_map.122 = f32[4,1,256]{2,1,0:T(1,128)} custom-call(f32[3,1,128]{2,1,0:T(1,128)} %bitcast.15, s32[1,128]{1,0:T(1,128)} %bitcast.18, s32[2,64]{1,0:T(2,128)} %bitcast.16, s32[1,2]{1,0:T(1,128)} %bitcast.19, s32[2,8]{1,0:T(2,128)} %bitcast.17, s32[1,1,1]{2,1,0:T(1,128)S(6)} %copy.14.total_hbm, f32[8,64]{1,0:T(8,128)} %radial_hbm.1, f32[8,64]{1,0:T(8,128)} %emb_hbm.1, ...), custom_call_target="tpu_custom_call" | custom-call | tf_op jit(solution)/shard_map/pallas_call | solution.py:630
  59.7 1.2 %negate_bitcast_fusion.1 = f32[1,1,1,256]{3,2,1,0:T(1,128)} fusion(f32[4,1,256]{2,1,0:T(1,128)} %shard_map.122), kind=kLoop, calls=%fused_computation.1 | loop fusion | flops 256 | bytes 2048 | tf_op jit(solution)/shard_map/neg | solution.py:690
  61.0 1.3 %negate_bitcast_fusion = f32[1,1,1,3,256]{4,2,3,1,0:T(1,128)} fusion(f32[4,1,256]{2,1,0:T(1,128)} %shard_map.122), kind=kLoop, calls=%fused_computation | loop fusion | flops 768 | bytes 6144

commit v3 on v2

--- a/solution.py
+++ b/solution.py
@@ -109,7 +109,6 @@
     env_grad,
     features,
     hidden,
-    slope,
     pull,
     push,
     send_sem,
@@ -125,7 +124,8 @@
         }
 
     far = [where for where in PLANE_FAR if where != (0, 0)]
-    around = [(a, b, c) for c in (-1, 1, 0) for a in (-1, 0, 1) for b in (-1, 0, 1)]
+    around = [(a, b, c) for a in (-1, 1, 0) for b in (-1, 0, 1) for c in (-1, 1)]
+    around += [(a, b, 0) for a in (-1, 1, 0) for b in (-1, 0, 1)]
     around.remove((0, 0, 0))
 
     barrier = pltpu.get_barrier_semaphore()
@@ -459,26 +459,28 @@
         features[rows, 128:256] = high.astype(BF16)
 
     load_first.wait()
-    before = contract(features[...], w_first[...], ((1,), (0,)))
-    gate = 0.5 + 0.5 * jnp.tanh(0.5 * before)
-    value = before * gate
-    hidden[...] = value.astype(BF16)
-    slope[...] = gate + value * (1.0 - gate)
     load_second.wait()
-    before = contract(hidden[...], w_second[...], ((1,), (0,)))
-    gate = 0.5 + 0.5 * jnp.tanh(0.5 * before)
-    value = before * gate
-    hidden[...] = value.astype(BF16)
-
     load_out.wait()
     w_out_parts = [part.astype(F32) for part in three_parts(out_ref[...])]
-    turn = ((gate + value * (1.0 - gate)) * w_out_parts[0]).astype(BF16)
-    turn = contract(turn, w_second[...], ((1,), (1,)))
-    turn = (turn * slope[...]).astype(BF16)
-    turn = contract(turn, w_first[...], ((1,), (1,)))
+    turns = []
     for h in range(2):
-        even = turn[2 * h * TILE : (2 * h + 1) * TILE]
-        odd = turn[(2 * h + 1) * TILE : (2 * h + 2) * TILE]
+        rows = slice(2 * h * TILE, 2 * (h + 1) * TILE)
+        before = contract(features[rows, :], w_first[...], ((1,), (0,)))
+        gate = 0.5 + 0.5 * jnp.tanh(0.5 * before)
+        value = before * gate
+        bend = gate + value * (1.0 - gate)
+        before = contract(value.astype(BF16), w_second[...], ((1,), (0,)))
+        gate = 0.5 + 0.5 * jnp.tanh(0.5 * before)
+        value = before * gate
+        hidden[rows, :] = value.astype(BF16)
+
+        turn = ((gate + value * (1.0 - gate)) * w_out_parts[0]).astype(BF16)
+        turn = contract(turn, w_second[...], ((1,), (1,)))
+        turn = (turn * bend).astype(BF16)
+        turns.append(contract(turn, w_first[...], ((1,), (1,))))
+    for h in range(2):
+        even = turns[h][:TILE]
+        odd = turns[h][TILE:]
         cols = slice(h * 128, (h + 1) * 128)
         pulls = [
             2.0 * jnp.where(left_half, even[:, 0:128], swap(odd[:, 0:128])),
@@ -534,7 +536,7 @@
                 push[axis, :, cols] = push[axis, :, cols] + flow
         return carry
 
-    lax.fori_loop(0, TILE // 8, backward, 0)
+    lax.fori_loop(0, TILE // 8, backward, 0, unroll=4)
 
     folded = []
     for axis in range(3):
@@ -629,7 +631,7 @@
     anywhere = pl.BlockSpec(memory_space=pltpu.HBM)
     both = pl.pallas_call(
         functools.partial(kernel, sizes),
-        out_shape=jax.ShapeDtypeStruct((4, 1, 4 * TILE), F32),
+        out_shape=pltpu.VMEM((4, 1, 4 * TILE), F32),
         in_specs=[anywhere] * 11,
         out_specs=vmem,
         scratch_shapes=[
@@ -664,7 +666,6 @@
             pltpu.VMEM((HARM * TILE, 256), BF16),
             pltpu.VMEM((256, 256), BF16),
             pltpu.VMEM((256, hidden), BF16),
-            pltpu.VMEM((256, hidden), F32),
             pltpu.VMEM((4 * TILE, EDGE), F32),
             pltpu.VMEM((3, 8, EDGE), F32),
             pltpu.SemaphoreType.DMA((44,)),

time: 62.4 us -> 60 us (0.962)
  other arithmetic: 2.48 us -> 1.15 us
  Pallas kernels: 58.4 us -> 57.4 us
    pallas_call x1, Pallas kernels: 58.4 us -> 57.4 us  [local(): pl.pallas_call(functools.partial(kernel, sizes), out_shape=pltpu.VMEM((4,...]
    unnamed x1, other arithmetic: 1.26 us -> 0.58 us
    neg x1, other arithmetic: 1.22 us -> 0.56 us  [local(): -both[3].reshape(1, 1, 1, 4 * TILE)]
where the time goes in v3:
time: 60 us; the launch traced here: 59.8 us
  Pallas kernels  57.4 us (96%)
  between operations  1.29 us (2%)
  other arithmetic  1.15 us (2%)
    pallas_call x1, Pallas kernels, local(): pl.pallas_call(functools.partial(kernel, sizes), out_shape=pltpu.VMEM((4,...  57.4 us

profile of v3, /device:TPU:1, one launch (start us, length us, event | category | flops | bytes accessed | tf_op | source)
XLA Modules:
  0.0 59.8 jit_solution(1917570642380551242)
XLA Ops:
  1.3 57.4 %shard_map.122 = f32[4,1,256]{2,1,0:T(1,128)S(1)} custom-call(f32[3,1,128]{2,1,0:T(1,128)} %bitcast.15, s32[1,128]{1,0:T(1,128)} %bitcast.18, s32[2,64]{1,0:T(2,128)} %bitcast.16, s32[1,2]{1,0:T(1,128)} %bitcast.19, s32[2,8]{1,0:T(2,128)} %bitcast.17, s32[1,1,1]{2,1,0:T(1,128)S(6)} %copy.14.total_hbm, f32[8,64]{1,0:T(8,128)} %radial_hbm.1, f32[8,64]{1,0:T(8,128)} %emb_hbm.1, ...), custom_call_target="tpu_custom_call" | custom-call | tf_op jit(solution)/shard_map/pallas_call | solution.py:632
  58.7 0.6 negate_bitcast_fusion.1
  59.3 0.6 negate_bitcast_fusion
